TPU v7x, 32 devices: a whole 2x2x4 slice. The times are simulated.
32 devices in a mesh: seq: 8 (over z, y), head: 4 (over x, core).
Axes of the slice: x: 2, y: 2, z: 4, core: 2. Of those that a mesh axis runs over, the one named last changes fastest.
Arguments:
- mamba_inner: bfloat16 [1024, 3072], P('seq', 'head'), may hold values from -6 to 6
- mamba_groups: bfloat16 [1024, 512], P('seq'), may hold values from -6 to 6
- selective_gate: bfloat16 [1024, 3072], P('seq', 'head'), may hold values from -6 to 6
- step_raw: float32 [48, 1024], P('head', 'seq'), may hold values from -3 to 3
- step_bias: float32 [48], P('head'), may hold values from -0.5 to 0.5
- decay_log: float32 [48], P('head'), may hold values from -12 to -2
- conv_inner: float32 [4, 3072], P(None, 'head'), may hold values from -3 to 3
- conv_groups: float32 [4, 512], replicated, may hold values from -3 to 3
- gated_norm_gain: float32 [3072], P('head'), may hold values from 0.1 to 1.9
- query_rows: bfloat16 [1024, 1024], P('seq', 'head'), may hold values from -8 to 8
- key_rows: bfloat16 [1024, 256], P('seq'), may hold values from -8 to 8
- value_rows: bfloat16 [1024, 256], P('seq'), may hold values from -6 to 6
- segment_ids: int32 [1024], P('seq'), may hold values from 0 to 15, never falling along the last dimension, each value on 1 to 682 neighbouring positions
- mamba_proj: bfloat16 [3072, 2048], P('head'), may hold values from -0.109375 to 0.109375
- attn_proj: bfloat16 [1024, 2048], P('head'), may hold values from -0.1875 to 0.1875
Outputs:
- mixed: bfloat16 [1024, 2048], P('seq', 'head')
Inputs may be any that keep to these rules, and one draw needn't show every extreme that they name: `segment_ids`: prompt numbers never fall along the tokens; each prompt holds 1 to 682 tokens and one holds exactly 682.
All inputs are finite; a program needn't handle non-finite values.
Results may differ from a plain program's by a relative error of at most 0.015.
Values may be sent and summed in bfloat16 or wider, within the bound.
A program may use at most 128 MiB of HBM per device.

v0:
```python
import math
import jax
import jax.numpy as jnp
from jax import lax
from jax.sharding import PartitionSpec as P

HEAD_CHANNELS = 64
STATE_SIZE = 256
QH = 8
KVH = 2
HD = 128


def shifted(value, axis, steps):
    count = lax.axis_size(axis)
    first, last = (max(0, -steps), min(count, count - steps))
    return lax.ppermute(value, axis, [(source, source + steps) for source in range(first, last)])


def entering(array, axis, combine, identity):
    length, position = (lax.axis_size(axis), lax.axis_index(axis))
    everything = jax.tree.map(
        lambda part, kind: lax.all_gather(part.astype(kind), axis),
        array,
        (jnp.bfloat16, jnp.bfloat16),
    )
    start = jax.tree.map(
        lambda part, zero: jnp.broadcast_to(jnp.asarray(zero, part.dtype), part.shape),
        array,
        identity,
    )

    def turn(k, before):
        reached = k < position
        new = combine(
            before, jax.tree.map(lambda part, own: part[k].astype(own.dtype), everything, array)
        )
        return jax.tree.map(lambda a, b: jnp.where(reached, a, b), new, before)

    return lax.fori_loop(0, length, turn, start)


def conv_silu(rows, weight, segs, rim_rows, rim_segs):
    item_count = rows.shape[0]
    padded = jnp.concatenate([rim_rows.astype(jnp.float32), rows.astype(jnp.float32)], 0)
    seg_pad = jnp.concatenate([rim_segs, segs], 0)
    total = jnp.zeros(rows.shape, jnp.float32)
    for offset in range(weight.shape[0]):
        window = padded[offset : offset + item_count]
        keep = (seg_pad[offset : offset + item_count] == segs).astype(jnp.float32)
        total = total + weight[offset][None, :] * window * keep[:, None]
    return jax.nn.silu(total).astype(jnp.bfloat16)


def mamba_local(inner, groups, segs, steps, rates, prev_last):
    highest = lax.Precision.HIGHEST
    cumul = jnp.cumsum(-steps * rates[:, None], axis=1)
    read_b = groups[:, :STATE_SIZE]
    read_c = groups[:, STATE_SIZE:]
    intersection = jnp.dot(read_c, read_b.T, preferred_element_type=jnp.float32)
    order = jnp.arange(segs.shape[0], dtype=jnp.int32)
    live = (segs[:, None] == segs[None, :]) & (order[:, None] >= order[None, :])
    decays = jnp.exp(jnp.where(live[None], cumul[:, :, None] - cumul[:, None, :], -jnp.inf))
    mixing = intersection[None] * decays
    scaled = inner.astype(jnp.float32) * steps.T[:, :, None]
    output = jnp.einsum("htj,jhd->thd", mixing, scaled, precision=highest)
    tail = jnp.exp(cumul[:, -1:] - cumul) * (segs == segs[-1]).astype(jnp.float32)[None, :]
    local_state = jnp.einsum(
        "ht,thd,tn->hdn", tail, scaled, read_b.astype(jnp.float32), precision=highest
    )
    through = jnp.exp(cumul[:, -1]) * (segs[-1] == prev_last).astype(jnp.float32)
    return (output, through, local_state, cumul)


def mamba_incoming(output, incoming, groups, segs, cumul, prev_last):
    read_c = groups[:, STATE_SIZE:].astype(jnp.float32)
    joined = (segs == prev_last).astype(jnp.float32)
    from_carry = jnp.einsum("hdn,tn->thd", incoming, read_c, precision=lax.Precision.HIGHEST)
    return output + jnp.exp(cumul).T[:, :, None] * joined[:, None, None] * from_carry


def combine_states(earlier, later):
    return (earlier[0] * later[0], later[0][:, None, None] * earlier[1] + later[1])


def shards(
    mamba_inner,
    mamba_groups,
    selective_gate,
    step_raw,
    step_bias,
    decay_log,
    conv_inner,
    conv_groups,
    gated_norm_gain,
    query_rows,
    key_rows,
    value_rows,
    segment_ids,
    mamba_proj,
    attn_proj,
):
    item_count = segment_ids.shape[0]
    taps = conv_inner.shape[0]
    resident_heads = step_raw.shape[0]
    rim_inner, rim_groups, rim_marks = shifted(
        (
            mamba_inner[item_count - taps + 1 :],
            mamba_groups[item_count - taps + 1 :],
            segment_ids[item_count - taps + 1 :].astype(jnp.bfloat16),
        ),
        "seq",
        1,
    )
    rim_segs = rim_marks.astype(jnp.float32).astype(jnp.int32)
    prev_last = rim_segs[-1]
    inner_filtered = conv_silu(mamba_inner, conv_inner, segment_ids, rim_inner, rim_segs).reshape(
        item_count, resident_heads, HEAD_CHANNELS
    )
    groups_conv = conv_silu(mamba_groups, conv_groups, segment_ids, rim_groups, rim_segs)
    steps = jax.nn.softplus(step_raw + step_bias[:, None])
    rates = jnp.exp(decay_log)
    output, through, local_state, cumul = mamba_local(
        inner_filtered, groups_conv, segment_ids, steps, rates, prev_last
    )
    identity = (jnp.ones_like(through), jnp.zeros_like(local_state))
    carry_decay, carry_state = entering((through, local_state), "seq", combine_states, identity)
    selective_output = mamba_incoming(
        output, carry_state, groups_conv, segment_ids, cumul, prev_last
    )
    gated_values = selective_output * jax.nn.silu(selective_gate.astype(jnp.float32)).reshape(
        item_count, resident_heads, HEAD_CHANNELS
    )
    mean_square = jnp.mean(gated_values * gated_values, axis=-1, keepdims=True)
    normalized_rows = (
        (
            gated_values
            * lax.rsqrt(mean_square + 1e-05)
            * gated_norm_gain.reshape(resident_heads, HEAD_CHANNELS)
        )
        .astype(jnp.bfloat16)
        .reshape(item_count, resident_heads * HEAD_CHANNELS)
    )
    heads_here = query_rows.shape[1] // HD
    group_size = QH // KVH
    kv_index = lax.axis_index("head") * heads_here // group_size
    my_keys = lax.dynamic_slice_in_dim(key_rows, kv_index * HD, HD, 1)
    my_values = lax.dynamic_slice_in_dim(value_rows, kv_index * HD, HD, 1)
    marks = segment_ids.astype(jnp.bfloat16)
    block_start = lax.axis_index("seq") * item_count
    query_pos = block_start + jnp.arange(item_count, dtype=jnp.int32)
    queries = query_rows.reshape(item_count, heads_here, HD).transpose(1, 0, 2)
    scale = 1.0 / math.sqrt(HD)
    start_state = (
        jnp.full((heads_here, item_count), -1e30, jnp.float32),
        jnp.zeros((heads_here, item_count), jnp.float32),
        jnp.zeros((heads_here, item_count, HD), jnp.float32),
    )
    piece_keys = lax.all_gather(my_keys, "seq", axis=0, tiled=True)
    piece_values = lax.all_gather(my_values, "seq", axis=0, tiled=True)
    piece_marks = lax.all_gather(marks, "seq", axis=0, tiled=True)
    rows = piece_keys.shape[0]
    width = math.gcd(rows, item_count)
    blocks = rows // width

    def one_block(state, item):
        top, total, summed = state
        block_keys, block_values, block_marks, offset = item
        key_pos = offset * width + jnp.arange(width, dtype=jnp.int32)
        key_seg = block_marks.astype(jnp.float32).astype(jnp.int32)
        allowed = (
            (key_seg[None, :] == segment_ids[:, None])
            & (key_pos[None, :] <= query_pos[:, None])
            & (key_pos[None, :] >= 0)
        )
        scores = (
            jnp.einsum("hqd,kd->hqk", queries, block_keys, preferred_element_type=jnp.float32)
            * scale
        )
        scores = jnp.where(allowed[None], scores, -jnp.inf)
        new_top = jnp.maximum(top, jnp.max(scores, axis=-1))
        rescale = jnp.exp(top - new_top)
        weights = jnp.exp(scores - new_top[..., None])
        total = total * rescale + jnp.sum(weights, axis=-1)
        summed = summed * rescale[..., None] + jnp.einsum(
            "hqk,kd->hqd",
            weights.astype(jnp.bfloat16),
            block_values,
            preferred_element_type=jnp.float32,
        )
        return ((new_top, total, summed), None)

    items = (
        piece_keys.reshape(blocks, width, HD),
        piece_values.reshape(blocks, width, HD),
        piece_marks.reshape(blocks, width),
        jnp.arange(blocks, dtype=jnp.int32),
    )
    result, unused = lax.scan(one_block, start_state, items)
    top_final, total_final, summed_final = result
    attended = (
        (summed_final / total_final[..., None])
        .astype(jnp.bfloat16)
        .transpose(1, 0, 2)
        .reshape(item_count, heads_here * HD)
    )
    terms = jnp.dot(normalized_rows, mamba_proj, preferred_element_type=jnp.float32) + jnp.dot(
        attended, attn_proj, preferred_element_type=jnp.float32
    )
    return lax.psum_scatter(terms.astype(jnp.bfloat16), "head", scatter_dimension=1, tiled=True)


def solution(mesh):
    placed = (
        P("seq", "head"),
        P("seq", None),
        P("seq", "head"),
        P("head", "seq"),
        P("head"),
        P("head"),
        P(None, "head"),
        P(),
        P("head"),
        P("seq", "head"),
        P("seq", None),
        P("seq", None),
        P("seq"),
        P("head", None),
        P("head", None),
    )
    return jax.shard_map(
        shards, mesh=mesh, in_specs=placed, out_specs=P("seq", "head"), check_vma=False
    )
```

profile of v0, /device:TPU:0, one launch (start us, length us, event | category | flops | bytes accessed | tf_op | source)
XLA Modules:
  0.0 241.9 jit_solution(1705443980735956197)
XLA Ops:
  7.9 5.4 %collective-permute-start.1 = (bf16[3]{0:T(256)(128)(2,1)}, bf16[3]{0:T(256)(128)(2,1)}, u32[]{:S(2)}, u32[]{:S(2)}) collective-permute-start(bf16[3]{0:T(256)(128)(2,1)} %slice.85), channel_id=1, source_target_pairs={{0,4},{4,8},{8,12},{12,16},{16,20},{20,24},{24,28},{1,5},{5,9},{9,... | collective-permute-start | bytes 26 | tf_op jit(solution)/shard_map/ppermute | solution.py:17
  14.0 3.5 %collective-permute-start.2 = (bf16[3,512]{1,0:T(4,128)(2,1)S(1)}, bf16[3,512]{1,0:T(4,128)(2,1)}, u32[]{:S(2)}, u32[]{:S(2)}) collective-permute-start(bf16[3,512]{1,0:T(4,128)(2,1)S(1)} %slice.95), channel_id=1, source_target_pairs={{0,4},{4,8},{8,12},{12,16},{16,20},{20,24},{24,28},{1,5},{5,9},{9,... | collective-permute-start | bytes 9224 | tf_op jit(solution)/shard_map/ppermute | solution.py:17
  19.1 3.5 %collective-permute-start = (bf16[3,768]{0,1:T(8,128)(2,1)}, bf16[3,768]{0,1:T(8,128)(2,1)}, u32[]{:S(2)}, u32[]{:S(2)}) collective-permute-start(bf16[3,768]{0,1:T(8,128)(2,1)} %copy.27), channel_id=1, source_target_pairs={{0,4},{4,8},{8,12},{12,16},{16,20},{20,24},{24,28},{1,5},{5,9},{9,... | collective-permute-start | bytes 13832 | tf_op jit(solution)/shard_map/ppermute | solution.py:17
  22.6 1.2 slice.106
  23.8 1.6 convert_element_type.131
  25.5 1.1 copy.28
  31.8 32.9 %all_gather.23 = bf16[1024,128]{1,0:T(8,128)(2,1)} all-gather(bf16[128,128]{1,0:T(8,128)(2,1)S(1)} %constant_dynamic-slice_fusion.2), channel_id=1, replica_groups=mesh['seq'=8,'head'=4] {'seq'}, dimensions={0}, use_global_device_ids=true | all-gather | bytes 294912 | tf_op jit(solution)/shard_map/all_gather | solution.py:159
  65.5 32.9 %all_gather.24 = bf16[1024,128]{1,0:T(8,128)(2,1)} all-gather(bf16[128,128]{1,0:T(8,128)(2,1)S(1)} %constant_dynamic-slice_fusion.1), channel_id=1, replica_groups=mesh['seq'=8,'head'=4] {'seq'}, dimensions={0}, use_global_device_ids=true | all-gather | bytes 294912 | tf_op jit(solution)/shard_map/all_gather | solution.py:160
  98.4 16.8 %all-gather.2 = bf16[8,1,128]{2,1,0:T(2,128)(2,1)S(1)} all-gather(bf16[1,1,128]{2,1,0:T(2,128)(2,1)S(1)} %get-tuple-element.295), channel_id=1, replica_groups=mesh['seq'=8,'head'=4] {'seq'}, dimensions={0}, use_global_device_ids=true | all-gather | bytes 2304 | tf_op jit(solution)/shard_map/all_gather | solution.py:161
  118.8 2.0 compare_convert_fusion.4
  122.1 1.6 multiply_convert_fusion.2
  124.7 2.5 %multiply_convert_fusion.1 = bf16[128,768]{0,1:T(8,128)(2,1)S(1)} fusion(f32[128,768]{0,1:T(8,128)} %convert_element_type.121, f32[3,768]{0,1:T(8,128)S(1)} %convert_element_type.120, f32[768]{0:T(1024)S(1)} %get-tuple-element.241, f32[128]{0:T(128)S(1)} %get-tuple-element.290, f32[768]{0:T(1024)S(1)} %get-tuple-element.242, f32[128]{0:T(128)S(1)} %get-tuple-element.291, ...), kind=kLoop, calls=%fused_computation.74 | loop fusion | flops 1769472 | bytes 612864 | tf_op jit(solution)/shard_map/convert_element_type | solution.py:52
  127.9 1.2 convolution_convert_fusion
  129.2 32.5 %while.30 = (s32[]{:T(128)}, f32[2,128]{1,0:T(2,128)S(1)}, f32[2,128]{1,0:T(2,128)S(1)}, f32[2,128,128]{2,1,0:T(8,128)S(1)}, bf16[8,128]{1,0:T(8,128)(2,1)}, /*i...) while((s32[]{:T(128)}, f32[2,128]{1,0:T(2,128)S(1)}, ...), condition=%wide.region_7.8_spmd.clone, body=%wide.region_4.7_spmd.clone.sunk | while | flops 17172484 | bytes 840889 | solution.py:199
  161.7 1.8 copy.29
  164.3 1.3 dynamic-slice
  166.4 1.8 convert_multiply_fusion
  168.2 2.6 %fusion.76 = f32[128,2048]{1,0:T(8,128)} fusion(bf16[128,256]{0,1:T(8,128)(2,1)S(1)} %bitcast.93, bf16[256,2048]{1,0:T(8,128)(2,1)} %param.33), kind=kOutput, calls=%fused_computation.132 | convolution fusion | flops 134217728 | bytes 2162688 | tf_op jit(solution)/shard_map/dot_general | solution.py:207
  172.5 18.7 %all-reduce = bf16[96]{0:T(256)(128)(2,1)S(1)} all-reduce(bf16[96]{0:T(256)(128)(2,1)S(1)} %dynamic-update-slice), channel_id=2, replica_groups=mesh['seq'=8,'head'=4] {'seq'}, use_global_device_ids=true, to_apply=%add | all-reduce | flops 96 | bytes 384
  191.4 18.2 %while.29 = (s32[]{:T(128)}, f32[12,64,256]{2,1,0:T(8,128)}, s32[]{:T(128)}, bf16[8,12]{1,0:T(8,128)(2,1)S(1)}, bf16[8,12,64,256]{3,2,1,0:T(8,128)(2,1)}, /*index=5*/s32[]{:T(128)}, s32[]{:T(128)}) while((s32[]{:T(128)}, f32[12,64,256]{2,1,0:T(8,128)}, s32[]{:T(128)}, bf16[8,12]{1,0:T(8,128)(2,1)S(1)}, ...), condition=%wide.region_2.3_spmd.clone, body=%wide.region_1.2_spmd.clone.sunk | while | flops 983056 | bytes 1966305 | solution.py:40
  191.5 2.1 fusion.92
  193.5 2.3 fusion.92
  195.8 2.3 fusion.92
  198.1 2.3 fusion.92
  200.4 2.3 fusion.92
  202.7 2.3 fusion.92
  205.0 2.3 fusion.92
  207.3 2.3 fusion.92
  209.6 1.7 convolution_multiply_fusion.1
  211.3 2.8 %multiply_reduce_fusion = (f32[128,12]{0,1:T(8,128)S(1)}, f32[128,12,64]{0,2,1:T(8,128)S(1)}) fusion(f32[128,12,64]{0,2,1:T(8,128)} %bitcast.92, f32[128,12,64]{0,2,1:T(8,128)S(1)} %convolution_multiply_fusion.1, f32[12,128]{1,0:T(8,128)S(1)} %reduce_window_sum.11, f32[128,128]{1,0:T(8,128)S(1)} %fusion.66, pred[128,128]{1,0:T(8,128)(4,1)S(1)} %fusion.64, ...), kind=kOutput, calls=%fused_computation.69 | convolution fusion | flops 152173056 | bytes 1476608 | tf_op jit(solution)/shard_map/htj,jhd->thd/dot_general | solution.py:66
  214.4 1.4 fusion.20
  215.8 19.3 %reduce-scatter.2.cloned.1.call-done = bf16[128,512]{1,0:T(8,128)(2,1)} async-done(((bf16[128,2048]{1,0:T(8,128)(2,1)}), bf16[128,512]{1,0:T(8,128)(2,1)}) %reduce-scatter.2.cloned.1.call-update) | async-done | bytes 131088 | tf_op jit(solution)/shard_map/reduce_scatter | solution.py:210
  (165 shorter events, 45.4 us)
Async XLA Ops:
  6.5 207.8 %copy-start = (bf16[768,2048]{1,0:T(8,128)(2,1)S(1)}, bf16[768,2048]{1,0:T(8,128)(2,1)}, u32[]{:S(2)}) copy-start(bf16[768,2048]{1,0:T(8,128)(2,1)} %param.32) | copy-start | bytes 9437188
  6.5 122.6 %copy-start.5 = (s32[128]{0:T(128)S(1)}, s32[128]{0:T(128)}, u32[]{:S(2)}) copy-start(s32[128]{0:T(128)} %param.31) | copy-start | bytes 1540
  6.5 184.9 %all-gather.5.cloned.1.call-start = ((), (), s32[]{:S(2)}) async-start(), calls=%async_computation.2 | async-start | bytes 3538944 | tf_op jit(solution)/shard_map/all_gather | solution.py:23
  7.9 108.9 %collective-permute-start.1 = (bf16[3]{0:T(256)(128)(2,1)}, bf16[3]{0:T(256)(128)(2,1)}, u32[]{:S(2)}, u32[]{:S(2)}) collective-permute-start(bf16[3]{0:T(256)(128)(2,1)} %slice.85), channel_id=1, source_target_pairs={{0,4},{4,8},{8,12},{12,16},{16,20},{20,24},{24,28},{1,5},{5,9},{9,... | collective-permute-start | bytes 26 | tf_op jit(solution)/shard_map/ppermute | solution.py:17
  14.0 107.4 %collective-permute-start.2 = (bf16[3,512]{1,0:T(4,128)(2,1)S(1)}, bf16[3,512]{1,0:T(4,128)(2,1)}, u32[]{:S(2)}, u32[]{:S(2)}) collective-permute-start(bf16[3,512]{1,0:T(4,128)(2,1)S(1)} %slice.95), channel_id=1, source_target_pairs={{0,4},{4,8},{8,12},{12,16},{16,20},{20,24},{24,28},{1,5},{5,9},{9,... | collective-permute-start | bytes 9224 | tf_op jit(solution)/shard_map/ppermute | solution.py:17
  19.1 104.6 %collective-permute-start = (bf16[3,768]{0,1:T(8,128)(2,1)}, bf16[3,768]{0,1:T(8,128)(2,1)}, u32[]{:S(2)}, u32[]{:S(2)}) collective-permute-start(bf16[3,768]{0,1:T(8,128)(2,1)} %copy.27), channel_id=1, source_target_pairs={{0,4},{4,8},{8,12},{12,16},{16,20},{20,24},{24,28},{1,5},{5,9},{9,... | collective-permute-start | bytes 13832 | tf_op jit(solution)/shard_map/ppermute | solution.py:17
  30.6 98.6 %copy-start.6 = (f32[128,12]{0,1:T(8,128)}, f32[128,12]{0,1:T(8,128)S(1)}, u32[]{:S(2)}) copy-start(f32[128,12]{0,1:T(8,128)S(1)} %get-tuple-element.281) | copy-start | bytes 18436
  123.7 3.5 %copy-start.2 = (bf16[128,512]{1,0:T(8,128)(2,1)}, bf16[128,512]{1,0:T(8,128)(2,1)S(1)}, u32[]{:S(2)}) copy-start(bf16[128,512]{1,0:T(8,128)(2,1)S(1)} %multiply_convert_fusion.2) | copy-start | bytes 393220
  127.2 0.7 copy-start.4
  127.2 36.3 %copy-start.10 = (f32[768]{0:T(1024)S(1)}, f32[768]{0:T(1024)}, u32[]{:S(2)}) copy-start(f32[768]{0:T(1024)} %param.27) | copy-start | bytes 9220
  129.1 106.0 %reduce-scatter.2.cloned.1.call-start = ((), (), s32[]{:S(2)}) async-start(), calls=%async_computation.1 | async-start | bytes 655360 | tf_op jit(solution)/shard_map/reduce_scatter | solution.py:210
  161.7 29.6 %copy-start.3 = (bf16[128,512]{1,0:T(8,128)(2,1)S(1)}, bf16[128,512]{1,0:T(8,128)(2,1)}, u32[]{:S(2)}) copy-start(bf16[128,512]{1,0:T(8,128)(2,1)} %copy-done.2) | copy-start | bytes 393220
  191.4 18.2 %copy-start.8 = (f32[128,12]{0,1:T(8,128)S(1)}, f32[128,12]{0,1:T(8,128)}, u32[]{:S(2)}) copy-start(f32[128,12]{0,1:T(8,128)} %get-tuple-element.283) | copy-start | bytes 18436
  191.4 19.9 %copy-start.7 = (f32[128,12]{0,1:T(8,128)S(1)}, f32[128,12]{0,1:T(8,128)}, u32[]{:S(2)}) copy-start(f32[128,12]{0,1:T(8,128)} %copy-done.6) | copy-start | bytes 18436
  191.4 22.7 %copy-start.9 = (f32[12,64]{1,0:T(8,128)S(1)}, f32[12,64]{1,0:T(8,128)}, u32[]{:S(2)}) copy-start(f32[12,64]{1,0:T(8,128)} %mul.345) | copy-start | bytes 9220
  209.6 4.7 %copy-start.1 = (f32[128,2048]{1,0:T(8,128)S(1)}, f32[128,2048]{1,0:T(8,128)}, u32[]{:S(2)}) copy-start(f32[128,2048]{1,0:T(8,128)} %fusion.76) | copy-start | bytes 3145732
Sparse Core Ops, SparseCore 0:
  129.2 58.6 all-gather.4
  215.9 19.1 reduce-scatter.1
where the time goes:
time: 244 us; the launch traced here: 242 us
  blocking collectives  101 us (41%)
  other arithmetic  41.5 us (17%)
  matrix products  25.3 us (10%)
  local copies, waits for them, and re-layouts  21.2 us (9%)
  waiting for transfers between devices  19.4 us (8%)
  between operations  15.7 us (6%)
  starting transfers between devices  12.4 us (5%)
  loops' own time  5.2 us (2%)
    all_gather x1, blocking collectives, shards(): piece_keys = lax.all_gather(my_keys, 'seq', axis=0, tiled=True)  32.9 us
    all_gather x1, blocking collectives, shards(): piece_values = lax.all_gather(my_values, 'seq', axis=0, tiled=True)  32.9 us
    reduce_scatter x1, waiting for transfers between devices, shards(): lax.psum_scatter(terms.astype(jnp.bfloat16), 'head', scatter_dimension=1,...  19.3 us
    unnamed x1, blocking collectives  18.7 us
    select_n x8, other arithmetic, turn(): return jax.tree.map(lambda a, b: jnp.where(reached, a, b), new, before)  18.1 us
    all_gather x1, blocking collectives, shards(): piece_marks = lax.all_gather(marks, 'seq', axis=0, tiled=True)  16.8 us
    ppermute x3, starting transfers between devices, shifted(): lax.ppermute(value, axis, [(source, source + steps) for source in range(f...  12.4 us
    dot_general x8, matrix products, one_block(): jnp.einsum('hqk,kd->hqd', weights.astype(jnp.bfloat16), block_values, pre...  7.87 us
  transfers between devices with their start and end apart: 5, of which 1 were waited for; matrix products, arithmetic and copies ran while one was open for 24% of the time, Pallas kernels for 0%

commit v1 on v0

--- a/solution.py
+++ b/solution.py
@@ -156,8 +156,11 @@
         jnp.zeros((heads_here, item_count), jnp.float32),
         jnp.zeros((heads_here, item_count, HD), jnp.float32),
     )
-    piece_keys = lax.all_gather(my_keys, "seq", axis=0, tiled=True)
-    piece_values = lax.all_gather(my_values, "seq", axis=0, tiled=True)
+    piece_keys, piece_values = jnp.split(
+        lax.all_gather(jnp.concatenate([my_keys, my_values], axis=1), "seq", axis=0, tiled=True),
+        [my_keys.shape[1]],
+        axis=1,
+    )
     piece_marks = lax.all_gather(marks, "seq", axis=0, tiled=True)
     rows = piece_keys.shape[0]
     width = math.gcd(rows, item_count)

time: 244 us -> 209 us (0.86)
  blocking collectives: 101 us -> 66.9 us
    all_gather x2 -> x1, blocking collectives: 65.8 us -> 31.4 us  [shards(): lax.all_gather(jnp.concatenate([my_keys, my_values], axis=1), 'seq', axis...]
  transfers between devices with their start and end apart: 5 -> 5, of which waited for: 1 -> 1; matrix products, arithmetic and copies ran while one was open for 24% -> 27% of each run, Pallas kernels for 0% -> 0%
where the time goes in v1:
time: 209 us; the launch traced here: 207 us
  blocking collectives  66.9 us (32%)
  other arithmetic  40.2 us (19%)
  matrix products  25.3 us (12%)
  local copies, waits for them, and re-layouts  21.3 us (10%)
  waiting for transfers between devices  19.7 us (9%)
  between operations  15.7 us (8%)
  starting transfers between devices  12.4 us (6%)
  loops' own time  5.2 us (2%)
    all_gather x1, blocking collectives, shards(): lax.all_gather(jnp.concatenate([my_keys, my_values], axis=1), 'seq', axis...  31.4 us
    reduce_scatter x1, waiting for transfers between devices, shards(): lax.psum_scatter(terms.astype(jnp.bfloat16), 'head', scatter_dimension=1,...  19.6 us
    unnamed x1, blocking collectives  18.3 us
    select_n x8, other arithmetic, turn(): return jax.tree.map(lambda a, b: jnp.where(reached, a, b), new, before)  18.1 us
    all_gather x1, blocking collectives, shards(): piece_marks = lax.all_gather(marks, 'seq', axis=0, tiled=True)  17.1 us
    ppermute x3, starting transfers between devices, shifted(): lax.ppermute(value, axis, [(source, source + steps) for source in range(f...  12.4 us
    dot_general x8, matrix products, one_block(): jnp.einsum('hqk,kd->hqd', weights.astype(jnp.bfloat16), block_values, pre...  7.86 us
    dot_general x8, matrix products, one_block(): jnp.einsum('hqd,kd->hqk', queries, block_keys, preferred_element_type=jnp...  7.61 us
  transfers between devices with their start and end apart: 5, of which 1 were waited for; matrix products, arithmetic and copies ran while one was open for 27% of the time, Pallas kernels for 0%

profile of v1, /device:TPU:0, one launch (start us, length us, event | category | flops | bytes accessed | tf_op | source)
XLA Modules:
  0.0 206.6 jit_solution(13640407440944146876)
XLA Ops:
  7.9 5.4 %collective-permute-start.1 = (bf16[3]{0:T(256)(128)(2,1)}, bf16[3]{0:T(256)(128)(2,1)}, u32[]{:S(2)}, u32[]{:S(2)}) collective-permute-start(bf16[3]{0:T(256)(128)(2,1)} %slice.85), channel_id=1, source_target_pairs={{0,4},{4,8},{8,12},{12,16},{16,20},{20,24},{24,28},{1,5},{5,9},{9,... | collective-permute-start | bytes 26 | tf_op jit(solution)/shard_map/ppermute | solution.py:17
  14.0 3.5 %collective-permute-start.2 = (bf16[3,512]{1,0:T(4,128)(2,1)S(1)}, bf16[3,512]{1,0:T(4,128)(2,1)}, u32[]{:S(2)}, u32[]{:S(2)}) collective-permute-start(bf16[3,512]{1,0:T(4,128)(2,1)S(1)} %slice.95), channel_id=1, source_target_pairs={{0,4},{4,8},{8,12},{12,16},{16,20},{20,24},{24,28},{1,5},{5,9},{9,... | collective-permute-start | bytes 9224 | tf_op jit(solution)/shard_map/ppermute | solution.py:17
  19.1 3.5 %collective-permute-start = (bf16[3,768]{0,1:T(8,128)(2,1)}, bf16[3,768]{0,1:T(8,128)(2,1)}, u32[]{:S(2)}, u32[]{:S(2)}) collective-permute-start(bf16[3,768]{0,1:T(8,128)(2,1)} %copy.27), channel_id=1, source_target_pairs={{0,4},{4,8},{8,12},{12,16},{16,20},{20,24},{24,28},{1,5},{5,9},{9,... | collective-permute-start | bytes 13832 | tf_op jit(solution)/shard_map/ppermute | solution.py:17
  22.6 1.2 slice.106
  23.8 1.6 convert_element_type.131
  25.5 1.1 copy.28
  31.9 31.4 %all_gather.20 = bf16[1024,256]{1,0:T(8,128)(2,1)S(1)} all-gather(bf16[128,256]{1,0:T(8,128)(2,1)S(1)} %pad_maximum_fusion.2), channel_id=1, replica_groups=mesh['seq'=8,'head'=4] {'seq'}, dimensions={0}, use_global_device_ids=true | all-gather | bytes 589824 | tf_op jit(solution)/shard_map/all_gather | solution.py:160
  64.1 17.1 %all-gather.2 = bf16[8,1,128]{2,1,0:T(2,128)(2,1)S(1)} all-gather(bf16[1,1,128]{2,1,0:T(2,128)(2,1)S(1)} %get-tuple-element.297), channel_id=1, replica_groups=mesh['seq'=8,'head'=4] {'seq'}, dimensions={0}, use_global_device_ids=true | all-gather | bytes 2304 | tf_op jit(solution)/shard_map/all_gather | solution.py:164
  84.2 1.3 compare_convert_fusion.4
  86.8 1.6 multiply_convert_fusion.2
  88.4 1.0 convert_element_type.120
  89.4 2.5 %multiply_convert_fusion.1 = bf16[128,768]{0,1:T(8,128)(2,1)S(1)} fusion(f32[128,768]{0,1:T(8,128)} %convert_element_type.121, f32[3,768]{0,1:T(8,128)S(1)} %convert_element_type.120, f32[768]{0:T(1024)S(1)} %get-tuple-element.241, f32[128]{0:T(128)S(1)} %get-tuple-element.292, f32[768]{0:T(1024)S(1)} %get-tuple-element.242, f32[128]{0:T(128)S(1)} %get-tuple-element.293, ...), kind=kLoop, calls=%fused_computation.74 | loop fusion | flops 1769472 | bytes 612864 | tf_op jit(solution)/shard_map/convert_element_type | solution.py:52
  92.6 1.2 convolution_convert_fusion
  93.9 32.5 %while.30 = (s32[]{:T(128)}, f32[2,128]{1,0:T(2,128)S(1)}, f32[2,128]{1,0:T(2,128)S(1)}, f32[2,128,128]{2,1,0:T(8,128)S(1)}, bf16[8,128]{1,0:T(8,128)(2,1)}, /*i...) while((s32[]{:T(128)}, f32[2,128]{1,0:T(2,128)S(1)}, ...), condition=%wide.region_7.8_spmd.clone, body=%wide.region_4.7_spmd.clone.sunk | while | flops 17172484 | bytes 840889 | solution.py:202
  126.4 1.8 copy.29
  129.0 1.3 dynamic-slice
  131.1 1.8 convert_multiply_fusion
  132.9 2.5 %fusion.77 = f32[128,2048]{1,0:T(8,128)} fusion(bf16[128,256]{0,1:T(8,128)(2,1)S(1)} %bitcast.93, bf16[256,2048]{1,0:T(8,128)(2,1)} %param.33), kind=kOutput, calls=%fused_computation.134 | convolution fusion | flops 134217728 | bytes 2162688 | tf_op jit(solution)/shard_map/dot_general | solution.py:210
  137.2 18.3 %all-reduce = bf16[96]{0:T(256)(128)(2,1)S(1)} all-reduce(bf16[96]{0:T(256)(128)(2,1)S(1)} %dynamic-update-slice), channel_id=2, replica_groups=mesh['seq'=8,'head'=4] {'seq'}, use_global_device_ids=true, to_apply=%add | all-reduce | flops 96 | bytes 384
  155.8 18.2 %while.29 = (s32[]{:T(128)}, f32[12,64,256]{2,1,0:T(8,128)}, s32[]{:T(128)}, bf16[8,12]{1,0:T(8,128)(2,1)S(1)}, bf16[8,12,64,256]{3,2,1,0:T(8,128)(2,1)}, /*index=5*/s32[]{:T(128)}, s32[]{:T(128)}) while((s32[]{:T(128)}, f32[12,64,256]{2,1,0:T(8,128)}, s32[]{:T(128)}, bf16[8,12]{1,0:T(8,128)(2,1)S(1)}, ...), condition=%wide.region_2.3_spmd.clone, body=%wide.region_1.2_spmd.clone.sunk | while | flops 983056 | bytes 1966305 | solution.py:40
  155.8 2.1 fusion.93
  157.9 2.3 %fusion.93 = f32[12,64,256]{2,1,0:T(8,128)} fusion(f32[12,64,256]{2,1,0:T(8,128)} %get-tuple-element.462, bf16[8,12,64,256]{3,2,1,0:T(8,128)(2,1)} %get-tuple-element.472, s32[]{:T(128)} %get-tuple-element.461, f32[12]{0:T(128)S(1)} %bitcast_convert_fusion.2, pred[]{:T(512)S(6)} %compare.8, pred[]{:T(512)S(6)} %lt.32), kind=kLoop, calls=%fused_computation.2.clone.1 | loop fusion | flops 983040 | bytes 1966134 | tf_op jit(solution)/shard_map/while/body/eval_jaxpr/jit(_where)/select_n | solution.py:38
  160.2 2.3 %fusion.93 = f32[12,64,256]{2,1,0:T(8,128)} fusion(f32[12,64,256]{2,1,0:T(8,128)} %get-tuple-element.462, bf16[8,12,64,256]{3,2,1,0:T(8,128)(2,1)} %get-tuple-element.472, s32[]{:T(128)} %get-tuple-element.461, f32[12]{0:T(128)S(1)} %bitcast_convert_fusion.2, pred[]{:T(512)S(6)} %compare.8, pred[]{:T(512)S(6)} %lt.32), kind=kLoop, calls=%fused_computation.2.clone.1 | loop fusion | flops 983040 | bytes 1966134 | tf_op jit(solution)/shard_map/while/body/eval_jaxpr/jit(_where)/select_n | solution.py:38
  162.5 2.3 %fusion.93 = f32[12,64,256]{2,1,0:T(8,128)} fusion(f32[12,64,256]{2,1,0:T(8,128)} %get-tuple-element.462, bf16[8,12,64,256]{3,2,1,0:T(8,128)(2,1)} %get-tuple-element.472, s32[]{:T(128)} %get-tuple-element.461, f32[12]{0:T(128)S(1)} %bitcast_convert_fusion.2, pred[]{:T(512)S(6)} %compare.8, pred[]{:T(512)S(6)} %lt.32), kind=kLoop, calls=%fused_computation.2.clone.1 | loop fusion | flops 983040 | bytes 1966134 | tf_op jit(solution)/shard_map/while/body/eval_jaxpr/jit(_where)/select_n | solution.py:38
  164.8 2.3 %fusion.93 = f32[12,64,256]{2,1,0:T(8,128)} fusion(f32[12,64,256]{2,1,0:T(8,128)} %get-tuple-element.462, bf16[8,12,64,256]{3,2,1,0:T(8,128)(2,1)} %get-tuple-element.472, s32[]{:T(128)} %get-tuple-element.461, f32[12]{0:T(128)S(1)} %bitcast_convert_fusion.2, pred[]{:T(512)S(6)} %compare.8, pred[]{:T(512)S(6)} %lt.32), kind=kLoop, calls=%fused_computation.2.clone.1 | loop fusion | flops 983040 | bytes 1966134 | tf_op jit(solution)/shard_map/while/body/eval_jaxpr/jit(_where)/select_n | solution.py:38
  167.1 2.3 %fusion.93 = f32[12,64,256]{2,1,0:T(8,128)} fusion(f32[12,64,256]{2,1,0:T(8,128)} %get-tuple-element.462, bf16[8,12,64,256]{3,2,1,0:T(8,128)(2,1)} %get-tuple-element.472, s32[]{:T(128)} %get-tuple-element.461, f32[12]{0:T(128)S(1)} %bitcast_convert_fusion.2, pred[]{:T(512)S(6)} %compare.8, pred[]{:T(512)S(6)} %lt.32), kind=kLoop, calls=%fused_computation.2.clone.1 | loop fusion | flops 983040 | bytes 1966134 | tf_op jit(solution)/shard_map/while/body/eval_jaxpr/jit(_where)/select_n | solution.py:38
  169.4 2.3 %fusion.93 = f32[12,64,256]{2,1,0:T(8,128)} fusion(f32[12,64,256]{2,1,0:T(8,128)} %get-tuple-element.462, bf16[8,12,64,256]{3,2,1,0:T(8,128)(2,1)} %get-tuple-element.472, s32[]{:T(128)} %get-tuple-element.461, f32[12]{0:T(128)S(1)} %bitcast_convert_fusion.2, pred[]{:T(512)S(6)} %compare.8, pred[]{:T(512)S(6)} %lt.32), kind=kLoop, calls=%fused_computation.2.clone.1 | loop fusion | flops 983040 | bytes 1966134 | tf_op jit(solution)/shard_map/while/body/eval_jaxpr/jit(_where)/select_n | solution.py:38
  171.7 2.3 %fusion.93 = f32[12,64,256]{2,1,0:T(8,128)} fusion(f32[12,64,256]{2,1,0:T(8,128)} %get-tuple-element.462, bf16[8,12,64,256]{3,2,1,0:T(8,128)(2,1)} %get-tuple-element.472, s32[]{:T(128)} %get-tuple-element.461, f32[12]{0:T(128)S(1)} %bitcast_convert_fusion.2, pred[]{:T(512)S(6)} %compare.8, pred[]{:T(512)S(6)} %lt.32), kind=kLoop, calls=%fused_computation.2.clone.1 | loop fusion | flops 983040 | bytes 1966134 | tf_op jit(solution)/shard_map/while/body/eval_jaxpr/jit(_where)/select_n | solution.py:38
  174.0 1.7 convolution_multiply_fusion.1
  175.7 2.8 %multiply_reduce_fusion = (f32[128,12]{0,1:T(8,128)S(1)}, f32[128,12,64]{0,2,1:T(8,128)S(1)}) fusion(f32[128,12,64]{0,2,1:T(8,128)} %bitcast.92, f32[128,12,64]{0,2,1:T(8,128)S(1)} %convolution_multiply_fusion.1, f32[12,128]{1,0:T(8,128)S(1)} %reduce_window_sum.11, f32[128,128]{1,0:T(8,128)S(1)} %fusion.66, pred[128,128]{1,0:T(8,128)(4,1)S(1)} %fusion.64, ...), kind=kOutput, calls=%fused_computation.69 | convolution fusion | flops 152173056 | bytes 1476608 | tf_op jit(solution)/shard_map/htj,jhd->thd/dot_general | solution.py:66
  178.7 1.4 fusion.20
  180.1 19.6 %reduce-scatter.2.cloned.1.call-done = bf16[128,512]{1,0:T(8,128)(2,1)} async-done(((bf16[128,2048]{1,0:T(8,128)(2,1)}), bf16[128,512]{1,0:T(8,128)(2,1)}) %reduce-scatter.2.cloned.1.call-update) | async-done | bytes 131088 | tf_op jit(solution)/shard_map/reduce_scatter | solution.py:213
  (165 shorter events, 43.8 us)
Async XLA Ops:
  6.5 172.2 %copy-start = (bf16[768,2048]{1,0:T(8,128)(2,1)S(1)}, bf16[768,2048]{1,0:T(8,128)(2,1)}, u32[]{:S(2)}) copy-start(bf16[768,2048]{1,0:T(8,128)(2,1)} %param.32) | copy-start | bytes 9437188
  6.5 77.6 %copy-start.5 = (s32[128]{0:T(128)S(1)}, s32[128]{0:T(128)}, u32[]{:S(2)}) copy-start(s32[128]{0:T(128)} %param.31) | copy-start | bytes 1540
  6.5 149.2 %all-gather.5.cloned.1.call-start = ((), (), s32[]{:S(2)}) async-start(), calls=%async_computation.2 | async-start | bytes 3538944 | tf_op jit(solution)/shard_map/all_gather | solution.py:23
  7.9 74.9 %collective-permute-start.1 = (bf16[3]{0:T(256)(128)(2,1)}, bf16[3]{0:T(256)(128)(2,1)}, u32[]{:S(2)}, u32[]{:S(2)}) collective-permute-start(bf16[3]{0:T(256)(128)(2,1)} %slice.85), channel_id=1, source_target_pairs={{0,4},{4,8},{8,12},{12,16},{16,20},{20,24},{24,28},{1,5},{5,9},{9,... | collective-permute-start | bytes 26 | tf_op jit(solution)/shard_map/ppermute | solution.py:17
  14.0 72.1 %collective-permute-start.2 = (bf16[3,512]{1,0:T(4,128)(2,1)S(1)}, bf16[3,512]{1,0:T(4,128)(2,1)}, u32[]{:S(2)}, u32[]{:S(2)}) collective-permute-start(bf16[3,512]{1,0:T(4,128)(2,1)S(1)} %slice.95), channel_id=1, source_target_pairs={{0,4},{4,8},{8,12},{12,16},{16,20},{20,24},{24,28},{1,5},{5,9},{9,... | collective-permute-start | bytes 9224 | tf_op jit(solution)/shard_map/ppermute | solution.py:17
  19.1 69.3 %collective-permute-start = (bf16[3,768]{0,1:T(8,128)(2,1)}, bf16[3,768]{0,1:T(8,128)(2,1)}, u32[]{:S(2)}, u32[]{:S(2)}) collective-permute-start(bf16[3,768]{0,1:T(8,128)(2,1)} %copy.27), channel_id=1, source_target_pairs={{0,4},{4,8},{8,12},{12,16},{16,20},{20,24},{24,28},{1,5},{5,9},{9,... | collective-permute-start | bytes 13832 | tf_op jit(solution)/shard_map/ppermute | solution.py:17
  30.6 63.3 %copy-start.6 = (f32[128,12]{0,1:T(8,128)}, f32[128,12]{0,1:T(8,128)S(1)}, u32[]{:S(2)}) copy-start(f32[128,12]{0,1:T(8,128)S(1)} %get-tuple-element.283) | copy-start | bytes 18436
  88.4 3.5 %copy-start.2 = (bf16[128,512]{1,0:T(8,128)(2,1)}, bf16[128,512]{1,0:T(8,128)(2,1)S(1)}, u32[]{:S(2)}) copy-start(bf16[128,512]{1,0:T(8,128)(2,1)S(1)} %multiply_convert_fusion.2) | copy-start | bytes 393220
  91.9 0.7 copy-start.4
  91.9 36.3 %copy-start.10 = (f32[768]{0:T(1024)S(1)}, f32[768]{0:T(1024)}, u32[]{:S(2)}) copy-start(f32[768]{0:T(1024)} %param.27) | copy-start | bytes 9220
  93.8 105.9 %reduce-scatter.2.cloned.1.call-start = ((), (), s32[]{:S(2)}) async-start(), calls=%async_computation.1 | async-start | bytes 655360 | tf_op jit(solution)/shard_map/reduce_scatter | solution.py:213
  126.4 29.2 %copy-start.3 = (bf16[128,512]{1,0:T(8,128)(2,1)S(1)}, bf16[128,512]{1,0:T(8,128)(2,1)}, u32[]{:S(2)}) copy-start(bf16[128,512]{1,0:T(8,128)(2,1)} %copy-done.2) | copy-start | bytes 393220
  155.8 18.2 %copy-start.8 = (f32[128,12]{0,1:T(8,128)S(1)}, f32[128,12]{0,1:T(8,128)}, u32[]{:S(2)}) copy-start(f32[128,12]{0,1:T(8,128)} %get-tuple-element.285) | copy-start | bytes 18436
  155.8 19.9 %copy-start.7 = (f32[128,12]{0,1:T(8,128)S(1)}, f32[128,12]{0,1:T(8,128)}, u32[]{:S(2)}) copy-start(f32[128,12]{0,1:T(8,128)} %copy-done.6) | copy-start | bytes 18436
  155.8 22.7 %copy-start.9 = (f32[12,64]{1,0:T(8,128)S(1)}, f32[12,64]{1,0:T(8,128)}, u32[]{:S(2)}) copy-start(f32[12,64]{1,0:T(8,128)} %mul.345) | copy-start | bytes 9220
  174.0 4.7 %copy-start.1 = (f32[128,2048]{1,0:T(8,128)S(1)}, f32[128,2048]{1,0:T(8,128)}, u32[]{:S(2)}) copy-start(f32[128,2048]{1,0:T(8,128)} %fusion.77) | copy-start | bytes 3145732
Sparse Core Ops, SparseCore 0:
  94.0 58.4 all-gather.4
  180.3 19.4 reduce-scatter.1
